TPU v7x, 32 devices: a whole 2x2x4 slice. The times are simulated.
32 devices in a mesh: dp: 8 (over z, x), tensor: 4 (over y, core).
Axes of the slice: x: 2, y: 2, z: 4, core: 2. Of those that a mesh axis runs over, the one named last changes fastest.
Arguments:
- inputs: bfloat16 [32, 196, 768], P('dp'), may hold values from -6 to 6
- target: bfloat16 [32, 196, 768], P('dp'), may hold values from -6 to 6
- valid: int32 [32, 196], P('dp'), may hold values from 0 to 1, as said below
- first_gain: float32 [768], replicated, may hold values from 0.5 to 1.5
- first_shift: float32 [768], replicated, may hold values from -3 to 3
- triple_weight: bfloat16 [3, 768, 768], P(None, 'dp', 'tensor'), may hold values from -0.21875 to 0.21875
- query_value_bias: float32 [2, 768], P(None, 'tensor'), may hold values from -3 to 3
- output_weight: bfloat16 [768, 768], P('tensor', 'dp'), may hold values from -0.875 to 0.875
- output_bias: float32 [768], replicated, may hold values from -3 to 3
- second_gain: float32 [768], replicated, may hold values from 0.5 to 1.5
- second_shift: float32 [768], replicated, may hold values from -3 to 3
- expand_weight: bfloat16 [768, 3072], P('dp', 'tensor'), may hold values from -0.21875 to 0.21875
- expand_bias: float32 [3072], P('tensor'), may hold values from -3 to 3
- shrink_weight: bfloat16 [3072, 768], P('tensor', 'dp'), may hold values from -0.109375 to 0.109375
- shrink_bias: float32 [768], replicated, may hold values from -3 to 3
- rows_table: float32 [27, 64], replicated, may hold values from -0.6 to 0.6
- columns_table: float32 [27, 64], replicated, may hold values from -0.6 to 0.6
Outputs:
- block_output: bfloat16 [32, 196, 768], P('dp')
- loss: float32 [], replicated
- input_grad: float32 [32, 196, 768], P('dp')
- first_gain_grad: float32 [768], replicated
- first_shift_grad: float32 [768], replicated
- triple_weight_grad: float32 [3, 768, 768], P(None, 'dp', 'tensor')
- query_value_bias_grad: float32 [2, 768], P(None, 'tensor')
- output_weight_grad: float32 [768, 768], P('tensor', 'dp')
- output_bias_grad: float32 [768], replicated
- second_gain_grad: float32 [768], replicated
- second_shift_grad: float32 [768], replicated
- expand_weight_grad: float32 [768, 3072], P('dp', 'tensor')
- expand_bias_grad: float32 [3072], P('tensor')
- shrink_weight_grad: float32 [3072, 768], P('tensor', 'dp')
- shrink_bias_grad: float32 [768], replicated
- rows_table_grad: float32 [27, 64], replicated
- columns_table_grad: float32 [27, 64], replicated
Inputs may be any that keep to these rules, and one draw needn't show every extreme that they name: `valid`: 1 marks an image token and 0 a padding token; the image tokens of a window fill a rectangle of its first rows and first columns, and every window holds at least one.
All inputs are finite; a program needn't handle non-finite values.
Results may differ from a plain program's by a relative error of at most 0.012.
Values may be sent and summed in bfloat16 or wider, within the bound.
A program may use at most 128 MiB of HBM per device.

v0:
```python
import math

import jax
import jax.numpy as jnp
import numpy as np
from jax import lax
from jax.experimental import pallas as pl
from jax.experimental.pallas import tpu as pltpu
from jax.sharding import PartitionSpec as P

MESH = pl.DeviceIdType.MESH

D = 768
HEADS = 12
HEAD = 64
WIN = 14
WIN_TOK = 196
MICRO = 2


def normalize(values):
    center = jnp.mean(values, axis=-1, keepdims=True)
    centered = values - center
    spread = jnp.mean(centered * centered, axis=-1, keepdims=True)
    inverse = lax.rsqrt(spread + 1e-06)
    return (centered * inverse, inverse)


def normalize_back(grad_out, unit, inverse, gain):
    scaled = grad_out * gain
    mean_one = jnp.mean(scaled, axis=-1, keepdims=True)
    mean_two = jnp.mean(scaled * unit, axis=-1, keepdims=True)
    return inverse * (scaled - mean_one - unit * mean_two)


def position_select(side):
    shape = (side, side, 2 * side - 1)
    first = lax.broadcasted_iota(jnp.int32, shape, 0)
    second = lax.broadcasted_iota(jnp.int32, shape, 1)
    slots = lax.broadcasted_iota(jnp.int32, shape, 2)
    return (slots == first - second + side - 1).astype(jnp.bfloat16)


def score_block(queries, keys, table_rows, table_cols, scale_factor):
    groups = queries.shape[0]
    side = queries.shape[1]
    heads = queries.shape[3]
    along_rows = jnp.einsum(
        "gabnc,aec->gnabe", queries, table_rows, preferred_element_type=jnp.float32
    )
    along_cols = jnp.einsum(
        "gabnc,bfc->gnabf", queries, table_cols, preferred_element_type=jnp.float32
    )
    scores = (
        jnp.einsum("gabnc,gefnc->gnabef", queries, keys, preferred_element_type=jnp.float32)
        * scale_factor
    )
    scores = scores + along_rows[..., :, None] + along_cols[..., None, :]
    return scores.reshape(groups, heads, side * side, side * side)


def gelu_exact(inner):
    return jax.nn.gelu(inner, approximate=False)


def row_total(partial_value):
    return lax.psum(partial_value, "tensor")


def share_of(values):
    share_rows = values.shape[0] // lax.axis_size("tensor")
    return lax.dynamic_slice_in_dim(values, lax.axis_index("tensor") * share_rows, share_rows, 0)


def shards(
    inputs,
    target,
    valid,
    first_gain,
    first_shift,
    triple_weight,
    query_value_bias,
    output_weight,
    output_bias,
    second_gain,
    second_shift,
    expand_weight,
    expand_bias,
    shrink_weight,
    shrink_bias,
    rows_table,
    columns_table,
):
    local_heads = HEADS // lax.axis_size("tensor")
    local_width = local_heads * HEAD
    local_windows = inputs.shape[0]
    win_micro = local_windows // MICRO
    micro_rows = win_micro * WIN_TOK
    scale_factor = 1.0 / math.sqrt(HEAD)
    highest = lax.Precision.HIGHEST
    live = valid.astype(jnp.float32)
    select = position_select(WIN)
    table_rows = jnp.einsum(
        "aej,jc->aec", select, rows_table.astype(jnp.bfloat16), preferred_element_type=jnp.float32
    ).astype(jnp.bfloat16)
    table_cols = jnp.einsum(
        "aej,jc->aec",
        select,
        columns_table.astype(jnp.bfloat16),
        preferred_element_type=jnp.float32,
    ).astype(jnp.bfloat16)
    rows_float = table_rows.astype(jnp.float32)
    cols_float = table_cols.astype(jnp.float32)
    triple_bias = jnp.stack(
        [query_value_bias[0], jnp.zeros_like(query_value_bias[0]), query_value_bias[1]]
    )
    saved = []
    outputs = []
    local_loss = jnp.zeros((), jnp.float32)
    for micro in range(MICRO):
        gathered = (
            lax.all_gather(triple_weight, "dp", axis=1, tiled=True),
            lax.all_gather(output_weight, "dp", axis=1, tiled=True),
            lax.all_gather(expand_weight, "dp", axis=0, tiled=True),
            lax.all_gather(shrink_weight, "dp", axis=1, tiled=True),
        )
        full_triple, full_output, full_expand, full_shrink = gathered
        lower = micro * win_micro
        flat_rows = inputs[lower : lower + win_micro].reshape(micro_rows, D).astype(jnp.float32)
        unit_one, inverse_one = normalize(flat_rows)
        normed = (unit_one * first_gain + first_shift).astype(jnp.bfloat16)
        projected = (
            jnp.einsum("rd,tde->rte", normed, full_triple, preferred_element_type=jnp.float32)
            + triple_bias
        )
        projected = projected.astype(jnp.bfloat16)
        split = projected.reshape(win_micro, WIN, WIN, 3, local_heads, HEAD)
        queries = split[:, :, :, 0]
        keys = split[:, :, :, 1]
        values = split[:, :, :, 2].reshape(win_micro, WIN_TOK, local_heads, HEAD)
        scores = score_block(queries, keys, table_rows, table_cols, scale_factor)
        peak = jnp.max(scores, axis=-1, keepdims=True)
        raised = jnp.exp(scores - peak)
        denominator = jnp.sum(raised, axis=-1, keepdims=True)
        log_total = peak + jnp.log(denominator)
        softmaxed = (raised / denominator).astype(jnp.bfloat16)
        mixed = jnp.einsum("gnqk,gknc->gqnc", softmaxed, values, preferred_element_type=jnp.float32)
        mixed = mixed.reshape(micro_rows, local_width).astype(jnp.bfloat16)
        partial_attended = jnp.dot(mixed, full_output, preferred_element_type=jnp.float32)
        middle = flat_rows + (row_total(partial_attended) + output_bias)
        unit_two, inverse_two = normalize(middle)
        normed_two = (unit_two * second_gain + second_shift).astype(jnp.bfloat16)
        before = jnp.dot(normed_two, full_expand, preferred_element_type=jnp.float32) + expand_bias
        hidden = gelu_exact(before).astype(jnp.bfloat16)
        partial_shrunk = jnp.dot(hidden, full_shrink, preferred_element_type=jnp.float32)
        result = middle + (row_total(partial_shrunk) + shrink_bias)
        aim = target[lower : lower + win_micro].reshape(micro_rows, D).astype(jnp.float32)
        marks = live[lower : lower + win_micro].reshape(micro_rows, 1)
        weighted_gap = marks * (result - aim)
        local_loss = local_loss + jnp.sum(weighted_gap * (result - aim))
        outputs.append(result.astype(jnp.bfloat16).reshape(win_micro, WIN_TOK, D))
        saved.append(
            (
                unit_one,
                inverse_one,
                normed,
                projected,
                log_total,
                mixed,
                unit_two,
                inverse_two,
                normed_two,
                before,
                hidden,
                weighted_gap,
            )
        )
    loss_total, count = lax.psum((local_loss, jnp.sum(live)), "dp")
    loss = loss_total / (count * D)
    grad_scale = local_windows * WIN_TOK * lax.axis_size("dp") / count
    triple_acc = jnp.zeros((3, D, local_width), jnp.float32)
    output_acc = jnp.zeros((local_width, D), jnp.float32)
    expand_acc = jnp.zeros((D, full_expand.shape[1]), jnp.float32)
    shrink_acc = jnp.zeros((full_shrink.shape[0], D), jnp.float32)
    first_gain_acc = jnp.zeros((D,), jnp.float32)
    first_shift_acc = jnp.zeros((D,), jnp.float32)
    second_gain_acc = jnp.zeros((D,), jnp.float32)
    second_shift_acc = jnp.zeros((D,), jnp.float32)
    output_bias_acc = jnp.zeros((D,), jnp.float32)
    shrink_bias_acc = jnp.zeros((D,), jnp.float32)
    expand_bias_acc = jnp.zeros((full_expand.shape[1],), jnp.float32)
    query_value_acc = jnp.zeros((2, local_width), jnp.float32)
    rows_expanded_acc = jnp.zeros((WIN, WIN, HEAD), jnp.float32)
    cols_expanded_acc = jnp.zeros((WIN, WIN, HEAD), jnp.float32)
    input_grads = []
    for micro in range(MICRO):
        gathered = (
            lax.all_gather(triple_weight, "dp", axis=1, tiled=True),
            lax.all_gather(output_weight, "dp", axis=1, tiled=True),
            lax.all_gather(expand_weight, "dp", axis=0, tiled=True),
            lax.all_gather(shrink_weight, "dp", axis=1, tiled=True),
        )
        full_triple, full_output, full_expand, full_shrink = gathered
        (
            unit_one,
            inverse_one,
            normed,
            projected,
            log_total,
            mixed,
            unit_two,
            inverse_two,
            normed_two,
            before,
            hidden,
            weighted_gap,
        ) = saved[micro]
        grad_result = grad_scale * weighted_gap
        shrink_bias_acc = shrink_bias_acc + jnp.sum(share_of(grad_result), axis=0)
        grad_result_low = grad_result.astype(jnp.bfloat16)
        shrink_acc = shrink_acc + jnp.einsum(
            "rf,rd->fd", hidden, grad_result_low, preferred_element_type=jnp.float32
        )
        grad_hidden = jnp.einsum(
            "rd,fd->rf", grad_result_low, full_shrink, preferred_element_type=jnp.float32
        )
        unused, gelu_pull = jax.vjp(gelu_exact, before)
        grad_before = gelu_pull(grad_hidden)[0].astype(jnp.bfloat16)
        expand_bias_acc = expand_bias_acc + jnp.sum(grad_before.astype(jnp.float32), axis=0)
        expand_acc = expand_acc + jnp.einsum(
            "rd,rf->df", normed_two, grad_before, preferred_element_type=jnp.float32
        )
        partial_two = jnp.einsum(
            "rf,df->rd", grad_before, full_expand, preferred_element_type=jnp.float32
        )
        grad_normed_two = row_total(partial_two)
        grad_middle = grad_result + normalize_back(
            grad_normed_two, unit_two, inverse_two, second_gain
        )
        second_gain_acc = second_gain_acc + jnp.sum(share_of(grad_normed_two * unit_two), axis=0)
        second_shift_acc = second_shift_acc + jnp.sum(share_of(grad_normed_two), axis=0)
        output_bias_acc = output_bias_acc + jnp.sum(share_of(grad_middle), axis=0)
        grad_middle_low = grad_middle.astype(jnp.bfloat16)
        output_acc = output_acc + jnp.einsum(
            "rc,rd->cd", mixed, grad_middle_low, preferred_element_type=jnp.float32
        )
        grad_mixed = jnp.einsum(
            "rd,cd->rc", grad_middle_low, full_output, preferred_element_type=jnp.float32
        )
        grad_mixed = grad_mixed.astype(jnp.bfloat16).reshape(win_micro, WIN_TOK, local_heads, HEAD)
        split = projected.reshape(win_micro, WIN, WIN, 3, local_heads, HEAD)
        queries = split[:, :, :, 0]
        keys = split[:, :, :, 1]
        queries_flat = queries.reshape(win_micro, WIN_TOK, local_heads, HEAD)
        keys_flat = keys.reshape(win_micro, WIN_TOK, local_heads, HEAD)
        values = split[:, :, :, 2].reshape(win_micro, WIN_TOK, local_heads, HEAD)
        scores = score_block(queries, keys, table_rows, table_cols, scale_factor)
        softmax_exact = jnp.exp(scores - log_total)
        grad_soft = jnp.einsum(
            "gqnc,gknc->gnqk", grad_mixed, values, preferred_element_type=jnp.float32
        )
        delta = jnp.sum(softmax_exact * grad_soft, axis=-1, keepdims=True)
        grad_scores = (softmax_exact * (grad_soft - delta)).astype(jnp.bfloat16)
        grad_values = jnp.einsum(
            "gnqk,gqnc->gknc",
            softmax_exact.astype(jnp.bfloat16),
            grad_mixed,
            preferred_element_type=jnp.float32,
        )
        grad_keys = (
            jnp.einsum(
                "gnqk,gqnc->gknc", grad_scores, queries_flat, preferred_element_type=jnp.float32
            )
            * scale_factor
        )
        grad_queries = (
            jnp.einsum(
                "gnqk,gknc->gqnc", grad_scores, keys_flat, preferred_element_type=jnp.float32
            )
            * scale_factor
        )
        grad_grid = grad_scores.astype(jnp.float32).reshape(
            win_micro, local_heads, WIN, WIN, WIN, WIN
        )
        row_part = jnp.sum(grad_grid, axis=5)
        col_part = jnp.sum(grad_grid, axis=4)
        queries_float = queries.astype(jnp.float32)
        rel_queries = jnp.einsum("gnabe,aec->gabnc", row_part, rows_float, precision=highest)
        rel_queries = rel_queries + jnp.einsum(
            "gnabf,bfc->gabnc", col_part, cols_float, precision=highest
        )
        grad_queries = grad_queries + rel_queries.reshape(win_micro, WIN_TOK, local_heads, HEAD)
        rows_expanded_acc = rows_expanded_acc + jnp.einsum(
            "gnabe,gabnc->aec", row_part, queries_float, precision=highest
        )
        cols_expanded_acc = cols_expanded_acc + jnp.einsum(
            "gnabf,gabnc->bfc", col_part, queries_float, precision=highest
        )
        grad_projected = jnp.stack(
            [
                grad_queries.reshape(micro_rows, local_width),
                grad_keys.reshape(micro_rows, local_width),
                grad_values.reshape(micro_rows, local_width),
            ],
            axis=1,
        ).astype(jnp.bfloat16)
        projected_float_sums = jnp.sum(grad_projected.astype(jnp.float32), axis=0)
        query_value_acc = query_value_acc + jnp.stack(
            [projected_float_sums[0], projected_float_sums[2]]
        )
        triple_acc = triple_acc + jnp.einsum(
            "rd,rte->tde", normed, grad_projected, preferred_element_type=jnp.float32
        )
        partial_one = jnp.einsum(
            "rte,tde->rd", grad_projected, full_triple, preferred_element_type=jnp.float32
        )
        grad_normed = row_total(partial_one)
        grad_tokens = grad_middle + normalize_back(grad_normed, unit_one, inverse_one, first_gain)
        first_gain_acc = first_gain_acc + jnp.sum(share_of(grad_normed * unit_one), axis=0)
        first_shift_acc = first_shift_acc + jnp.sum(share_of(grad_normed), axis=0)
        input_grads.append(grad_tokens.reshape(win_micro, WIN_TOK, D))
    select_float = select.astype(jnp.float32)
    rows_table_part = jnp.einsum("aej,aec->jc", select_float, rows_expanded_acc, precision=highest)
    cols_table_part = jnp.einsum("aej,aec->jc", select_float, cols_expanded_acc, precision=highest)
    triple_grad, output_grad, expand_grad, shrink_grad = (
        lax.psum_scatter(triple_acc, "dp", scatter_dimension=1, tiled=True),
        lax.psum_scatter(output_acc, "dp", scatter_dimension=1, tiled=True),
        lax.psum_scatter(expand_acc, "dp", scatter_dimension=0, tiled=True),
        lax.psum_scatter(shrink_acc, "dp", scatter_dimension=1, tiled=True),
    )
    over_heads = lax.psum(
        (
            rows_table_part,
            cols_table_part,
            first_gain_acc,
            first_shift_acc,
            output_bias_acc,
            second_gain_acc,
            second_shift_acc,
            shrink_bias_acc,
        ),
        "tensor",
    )
    summed_small = lax.psum(
        (
            over_heads[0],
            over_heads[1],
            over_heads[2],
            over_heads[3],
            over_heads[4],
            over_heads[5],
            over_heads[6],
            over_heads[7],
            query_value_acc,
            expand_bias_acc,
        ),
        "dp",
    )
    return (
        jnp.concatenate(outputs, axis=0),
        loss,
        jnp.concatenate(input_grads, axis=0),
        summed_small[2],
        summed_small[3],
        triple_grad,
        summed_small[8],
        output_grad,
        summed_small[4],
        summed_small[5],
        summed_small[6],
        expand_grad,
        summed_small[9],
        shrink_grad,
        summed_small[7],
        summed_small[0],
        summed_small[1],
    )


ROWS = 208
KEYS = 256
CHUNKS = ((0, 112), (112, 96))
F32 = jnp.float32
BF16 = jnp.bfloat16


def z_mate(z, k):
    if k == 0:
        return z
    if k == 1:
        return z + 1 - 2 * (z % 2)
    if k == 2:
        return (z + 2) % 4
    return 3 - z


def dot_nn(a, b):
    return lax.dot_general(a, b, (((1,), (0,)), ((), ())), preferred_element_type=F32)


def dot_nt(a, b):
    return lax.dot_general(a, b, (((1,), (1,)), ((), ())), preferred_element_type=F32)


def dot_tn(a, b):
    return lax.dot_general(a, b, (((0,), (0,)), ((), ())), preferred_element_type=F32)


def column_sum(values):
    return jnp.sum(values, axis=0, keepdims=True)


UNITS = ((0, 1, 2, 0, 0), (0, 1, 2, 1, 1), (3, 5, 6, 0, 1))


PLAN = (2, 1, 3, 0, 1, 4, 1, 1, 1, 6, 1, 2, 0, 1, 2, 0, 0, 0, 0, 2, 1, 1, 2, 0, 1, 0, 0, 4, 2)


def block_kernel(
    x_in,
    target_in,
    valid_hbm,
    gain1_hbm,
    shift1_hbm,
    triple_hbm,
    qv_bias_hbm,
    out_w_hbm,
    bias_out_hbm,
    gain2_hbm,
    shift2_hbm,
    we_hbm,
    expand_bias_hbm,
    ws_hbm,
    bias_shrink_hbm,
    rows_hbm,
    columns_hbm,
    block_out,
    grad_out,
    ga_out,
    ge_out,
    gs_out,
    small_out,
    table_out,
    valid_in,
    gain1_in,
    shift1_in,
    triple_in,
    qv_bias_in,
    out_w_in,
    bias_out_in,
    gain2_in,
    shift2_in,
    we_in,
    expand_bias_in,
    ws_in,
    bias_shrink_in,
    rows_in,
    columns_in,
    wa_in,
    wa,
    we,
    ws,
    xt,
    tt,
    onehot,
    place,
    pick,
    tabs,
    bo,
    ig,
    mix,
    ga,
    ge,
    gs,
    side,
    xf,
    unit1,
    unit2,
    inv1,
    inv2,
    mid,
    acc,
    n1,
    n2,
    gr,
    gm,
    pj,
    ps,
    mx,
    mxr,
    hid,
    hidr,
    slope,
    gb,
    gbr,
    gmx,
    gp,
    gpr,
    t2,
    tg,
    es,
    er,
    es3,
    er3,
    sums,
    shrink_row,
    gw,
    xs,
    xr,
    zs,
    zr,
    ps2,
    pr2,
    ptotal,
    pxs,
    pxr,
    cnt,
    cntr,
    sb,
    sbr,
    tb,
    tbr,
    load_sem,
    send_sem,
    recv_sem,
):
    dp = lax.axis_index("dp")
    t = lax.axis_index("tensor")
    z = dp // 2
    x = dp % 2
    y = t // 2
    c = t % 2
    z_mates = [(z_mate(z, k) * 2 + x, t) for k in (1, 2, 3)]
    x_mate = (z * 2 + 1 - x, t)
    y_mate = (dp, (1 - y) * 2 + c)
    c_mate = (dp, y * 2 + 1 - c)
    peer_window = (1 - y) * 2 + c
    token_total = lax.axis_size("dp") * 4 * WIN_TOK

    started = []

    def send(src, dst, mate):
        i = len(started)
        copy = pltpu.make_async_remote_copy(
            src_ref=src,
            dst_ref=dst,
            send_sem=send_sem.at[i],
            recv_sem=recv_sem.at[i],
            device_id=mate,
            device_id_type=MESH,
        )
        copy.start()
        started.append(copy)
        return copy

    barrier = pltpu.get_barrier_semaphore()
    for mate in z_mates + [x_mate, y_mate, c_mate]:
        pl.semaphore_signal(barrier, inc=1, device_id=mate, device_id_type=MESH)

    loads = []

    def load(src, dst):
        copy = pltpu.make_async_copy(src, dst, load_sem.at[len(loads)])
        copy.start()
        loads.append(copy)
        return copy

    first_loads = [load(triple_hbm, triple_in), load(out_w_hbm, out_w_in)]
    group_loads = [load(we_hbm, we_in), load(ws_hbm, ws_in)]
    x_load = load(x_in, xt)
    side_loads = [
        load(src, dst)
        for src, dst in (
            (expand_bias_hbm, expand_bias_in),
            (qv_bias_hbm, qv_bias_in),
            (valid_hbm, valid_in),
            (gain1_hbm, gain1_in),
            (shift1_hbm, shift1_in),
            (bias_out_hbm, bias_out_in),
            (gain2_hbm, gain2_in),
            (shift2_hbm, shift2_in),
            (bias_shrink_hbm, bias_shrink_in),
            (rows_hbm, rows_in),
            (columns_hbm, columns_in),
        )
    ]
    target_load = load(target_in, tt)

    w_in = (wa_in, we_in, ws_in)
    w_full = (wa, we, ws)
    from_z = {}
    from_x = {}
    from_p = {}
    from_c = {}

    def row_of(k, xx):
        return z_mate(z, k) * 2 + xx

    first = pl.ds(0, 640)
    last = pl.ds(640, 128)

    def gather_start(g):
        full = w_full[g]
        from_p[g, 0] = send(w_in[g].at[:, last], full.at[0, dp, :, last], x_mate)
        for k in (3, 1):
            from_z[g, k] = send(w_in[g].at[:, first], full.at[0, dp, :, first], z_mates[k - 1])
        from_x[g, 0] = send(w_in[g].at[:, first], full.at[0, dp, :, first], x_mate)
        from_c[g, 0] = send(w_in[g], full.at[1, dp], c_mate)
        full[0, dp] = w_in[g][...]

    def to_core(g, i, *at):
        from_c[g, i] = send(w_full[g].at[(0,) + at], w_full[g].at[(1,) + at], c_mate)

    def gather_pair(g, k):
        from_p[g, k].wait_recv()
        pair = (pl.ds(2 * z_mate(z, k), 2), slice(None), last)
        block = w_full[g].at[(0,) + pair]
        if k == 0:
            for m in (3, 1):
                from_p[g, m] = send(block, block, z_mates[m - 1])
            to_core(g, 8, row_of(0, 1 - x), slice(None), last)
        else:
            if k == 3:
                from_p[g, 2] = send(block, block, z_mates[0])
            to_core(g, 8 + k, *pair)

    def gather_z(g, k):
        from_z[g, k].wait_recv()
        block = w_full[g].at[0, row_of(k, x), :, first]
        if k == 3:
            from_z[g, 2] = send(block, block, z_mates[0])
        else:
            from_x[g, k] = send(block, block, x_mate)
        to_core(g, k, row_of(k, x), slice(None), first)

    def gather_far(g):
        block = w_full[g].at[0, row_of(3, x), :, first]
        from_x[g, 3] = send(block, block, x_mate)

    def gather_x(g, k):
        from_x[g, k].wait_recv()
        to_core(g, 4 + k, row_of(k, 1 - x), slice(None), first)

    def gather_end(g, far):
        for k in (2, 3, 6, 7, 10, 11) if far else (0, 1, 4, 5, 8, 9):
            from_c[g, k].wait_recv()

    tasks = []
    done = set()
    plan = iter(PLAN)

    def add(key, step, *args):
        tasks.append((key, step, args))

    def serve():
        key, step, args = tasks.pop(0)
        step(*args)
        done.add(key)

    def point():
        for _ in range(next(plan, 0)):
            if tasks:
                serve()

    def need(key):
        while key not in done:
            serve()

    def gather_add(g):
        add(("pair", g, 0), gather_pair, g, 0)
        add(("z", g, 3), gather_z, g, 3)
        if g == 0:
            add(("start", 1), gather_start, 1)
        add(("z", g, 1), gather_z, g, 1)
        add(("far", g), gather_far, g)
        add(("pair", g, 3), gather_pair, g, 3)
        add(("x", g, 0), gather_x, g, 0)
        add(("pair", g, 1), gather_pair, g, 1)
        add(("z", g, 2), gather_z, g, 2)
        if g == 0:
            add(("count",), count_spread)
            add(("start", 2), gather_start, 2)
        add(("x", g, 1), gather_x, g, 1)
        add(("near", g), gather_end, g, False)
        add(("x", g, 3), gather_x, g, 3)
        add(("pair", g, 2), gather_pair, g, 2)
        add(("x", g, 2), gather_x, g, 2)
        add(("all", g), gather_end, g, True)

    cnt_z = []

    def count_spread():
        cnt_x.wait_recv()
        cnt[1] = cnt[0] + cntr[0]
        cnt_z.extend(send(cnt.at[1], cntr.at[k], z_mates[k - 1]) for k in (1, 2, 3))

    for copy in first_loads:
        copy.wait()
    for i in range(3):
        wa_in[:, 128 * i : 128 * i + 128] = triple_in[i, :, 0:128]
    source = lax.broadcasted_iota(jnp.int32, (192, 256), 0)
    column = lax.broadcasted_iota(jnp.int32, (192, 256), 1)
    tail = sum(
        dot_nn(
            triple_in[i],
            ((source >= 128) & (source - 128 == column - 64 * i)).astype(F32).astype(BF16),
        )
        for i in range(3)
    )
    out_w = out_w_in[...]
    tail = tail + dot_tn(
        out_w, ((source >= 128) & (source + 64 == column)).astype(F32).astype(BF16)
    )
    wa_in[:, 384:640] = tail.astype(BF16)
    wa_in[:, 640:768] = dot_tn(
        out_w, (source == column).astype(F32).astype(BF16)[:, 0:128]
    ).astype(BF16)
    def fourteens(at):
        whole = jnp.floor((at + 0.5) * (1.0 / WIN))
        return whole, at - WIN * whole

    def grid(shape, dim):
        return lax.broadcasted_iota(jnp.int32, shape, dim).astype(F32)

    def entries(shape, dim):
        at = grid(shape, dim)
        side = (at >= 256.0).astype(F32)
        at = at - 256.0 * side
        main, other = fourteens(at)
        return side, main, other, at < float(WIN_TOK)

    side_of, main, other, valid = entries((512, 64), 0)
    slot = main - other + (WIN - 1) + 32.0 * side_of
    onehot[...] = jnp.where(valid & (grid((512, 64), 1) == slot), 1.0, 0.0).astype(BF16)
    side_of, main, other, valid = entries((ROWS, 512), 1)
    token = grid((ROWS, 512), 0)
    down, across = fourteens(token)
    hit = valid & (main == jnp.where(side_of > 0.5, across, down)) & (token < float(WIN_TOK))
    place[...] = jnp.where(hit, 1.0, 0.0)
    side_of, main, other, valid = entries((512, KEYS), 0)
    token = grid((512, KEYS), 1)
    down, across = fourteens(token)
    hit = valid & (other == jnp.where(side_of > 0.5, across, down)) & (token < float(WIN_TOK))
    pick[...] = jnp.where(hit, 1.0, 0.0).astype(BF16)
    pl.semaphore_wait(barrier, 6)
    gather_start(0)
    for copy in group_loads + side_loads:
        copy.wait()
    side[0] = jnp.zeros((8, D), F32)
    side[0, 0:1, :] = expand_bias_in[...].reshape(1, D)
    side[0, 1:2, 0:128] = qv_bias_in[0:1, 0:128]
    side[0, 1:2, 256:384] = qv_bias_in[1:2, 0:128]
    side[0, 1:2, 384:448] = qv_bias_in[0:1, 128:192]
    side[0, 1:2, 512:576] = qv_bias_in[1:2, 128:192]
    side_copy = send(side.at[0], side.at[1], c_mate)
    marks_all = valid_in[...].astype(F32)
    cnt[0] = jnp.full((8, 128), jnp.sum(marks_all), F32)
    cnt_x = send(cnt.at[0], cntr.at[0], x_mate)
    for g in range(3):
        gather_add(g)

    gain1 = gain1_in[...].reshape(1, D)
    shift1 = shift1_in[...].reshape(1, D)
    bias_out = bias_out_in[...].reshape(1, D)
    gain2 = gain2_in[...].reshape(1, D)
    shift2 = shift2_in[...].reshape(1, D)
    shrink_row[...] = bias_shrink_in[...].reshape(1, D)

    lane = lax.broadcasted_iota(jnp.int32, (1, 128), 1)
    half = ((lane < 64).astype(F32), (lane >= 64).astype(F32))
    key_mask = [(m * 0.125).astype(BF16) for m in half]
    half = [m.astype(BF16) for m in half]
    key_lane = lax.broadcasted_iota(jnp.int32, (1, KEYS), 1)
    key_bias = jnp.where(key_lane < WIN_TOK, 0.0, -1e30).astype(F32)

    row_ids = lax.broadcasted_iota(jnp.int32, (4, WIN_TOK), 0)
    own_marks = column_sum(jnp.where(row_ids == t, marks_all, 0.0))
    eye = lax.broadcasted_iota(jnp.int32, (ROWS, WIN_TOK), 0) == lax.broadcasted_iota(
        jnp.int32, (ROWS, WIN_TOK), 1
    )
    live = jnp.sum(jnp.where(eye, own_marks, 0.0), axis=1, keepdims=True)

    window_ids = lax.broadcasted_iota(jnp.int32, (1, 4, 1), 1)

    def window_of(ref, window):
        return jnp.sum(ref[...].astype(F32) * (window_ids == window).astype(F32), axis=1)

    xf[...] = jnp.zeros_like(xf)
    x_load.wait()
    for w in range(2):
        xf[w, 0:WIN_TOK, :] = window_of(xt, peer_window if w else t)
        point()
        unit, inverse = normalize(xf[w])
        n1[0, w] = (unit * gain1 + shift1).astype(BF16)
        if w == 0:
            unit1[...] = unit
            inv1[...] = inverse
    n1_copy = send(n1.at[0], n1.at[1], c_mate)
    tabs[...] = jnp.zeros_like(tabs)
    tabs[0:27, 0:64] = rows_in[...]
    tabs[32:59, 0:64] = columns_in[...]
    t2[0] = dot_nn(onehot[...], tabs[...].astype(BF16)).astype(BF16)
    t2[1] = dot_nn(onehot[...], pltpu.roll(tabs[...], 64, 1).astype(BF16)).astype(BF16)
    pj[:, :, ROWS:, :] = jnp.zeros((2, 2, KEYS - ROWS, 896), BF16)
    tg[...] = jnp.zeros_like(tg)

    def project(w):
        def body(j, carry):
            value = dot_nn(n1[0, w], wa[j, :, :, 0:640].reshape(D, 640)) + side[j, 1:2, 0:640]
            pj[w, j, 0:ROWS, 0:640] = value.astype(BF16)
            rolled = pltpu.roll(value[:, 384:512], 64, 1)
            pj[w, j, 0:ROWS, 640:768] = rolled.astype(BF16)
            rolled = pltpu.roll(value[:, 512:640], 64, 1)
            pj[w, j, 0:ROWS, 768:896] = rolled.astype(BF16)
            return carry

        lax.fori_loop(0, 2, body, 0)

    def unit_of(w, j, h):
        q, k, v, p, pv = UNITS[h]
        query = pj[w, j, 0:ROWS, 128 * q : 128 * q + 128]
        key = pj[w, j, :, 128 * k : 128 * k + 128] * key_mask[p]
        value = pj[w, j, :, 128 * v : 128 * v + 128] * half[pv]
        return query, key, value

    def attend(w):
        def body(j, carry):
            mixes = []
            for h in range(3):
                query, key, value = unit_of(w, j, h)
                along = dot_nt(query, t2[UNITS[h][3]]) * place[...]
                high = along.astype(BF16)
                low = (along - high.astype(F32)).astype(BF16)
                scores = dot_nt(query, key) + dot_nn(high, pick[...]) + dot_nn(low, pick[...])
                scores = scores + key_bias
                raised = jnp.exp(scores - jnp.max(scores, axis=-1, keepdims=True))
                soft = raised * (1.0 / jnp.sum(raised, axis=-1, keepdims=True))
                ps[w, j, h] = soft
                mixes.append(dot_nn(soft.astype(BF16), value))
            mx[j, w, :, 0:128] = mixes[2].astype(BF16)
            mx[j, w, :, 128:256] = (mixes[0] + mixes[1]).astype(BF16)
            return carry

        lax.fori_loop(0, 2, body, 0)
        point()

    def attended(w, lo, n):
        return dot_nt(mx[0, w, lo : lo + n, :], wa[0, :, :, 512:768].reshape(D, 256)) + dot_nt(
            mx[1, w, lo : lo + n, :], wa[1, :, :, 512:768].reshape(D, 256)
        )

    side_copy.wait_recv()
    need(("all", 0))
    project(1)
    point()
    attend(1)
    e1 = []
    for lo, n in CHUNKS:
        es[0, lo : lo + n, :] = attended(1, lo, n).astype(BF16)
        e1.append(send(es.at[0, pl.ds(lo, n)], er.at[0, pl.ds(lo, n)], y_mate))
    point()
    project(0)
    point()
    attend(0)
    mx_copy = send(mx.at[1], mxr, c_mate)
    mid[...] = xf[0] + bias_out + attended(0, 0, ROWS)
    point()

    e2 = []
    n2_c = []
    for i, (lo, n) in enumerate(CHUNKS):
        point()
        e1[i].wait_recv()
        middle = mid[lo : lo + n, :] + er[0, lo : lo + n, :].astype(F32)
        mid[lo : lo + n, :] = middle
        unit, inverse = normalize(middle)
        unit2[lo : lo + n, :] = unit
        inv2[lo : lo + n, :] = inverse
        n2[0, 0, lo : lo + n, :] = (unit * gain2 + shift2).astype(BF16)
        rows = pl.ds(lo, n)
        e2.append(send(n2.at[0, 0, rows], n2.at[0, 1, rows], y_mate))
        n2_c.append(send(n2.at[0, 0, rows], n2.at[1, 0, rows], c_mate))

    def feed(w, lo, n):
        def body(j, carry):
            before = dot_nn(n2[0, w, lo : lo + n, :], we[j].reshape(D, D)) + side[j, 0:1, :]
            phi = 0.5 * (1.0 + lax.erf(before * math.sqrt(0.5)))
            hid[j, w, lo : lo + n, :] = (before * phi).astype(BF16)
            bell = jnp.exp(-0.5 * before * before) * (1.0 / math.sqrt(2.0 * math.pi))
            slope[j, w, lo : lo + n, :] = phi + before * bell
            return carry

        lax.fori_loop(0, 2, body, 0)
        point()

    zone = z // 2
    zones = (zone, 1 - zone)
    halves = [pl.ds(pl.multiple_of(q * 384, 128), 384) for q in zones]

    def shrunk(w, i):
        rows = pl.ds(zones[i] * 4, 4)
        return dot_nt(hid[0, w], ws[0, rows].reshape(384, D)) + dot_nt(
            hid[1, w], ws[1, rows].reshape(384, D)
        )

    need(("all", 1))
    for lo, n in CHUNKS:
        feed(0, lo, n)
    for i, (lo, n) in enumerate(CHUNKS):
        rows = pl.ds(lo, n)
        point()
        e2[i].wait_recv()
        n2_c.append(send(n2.at[0, 1, rows], n2.at[1, 1, rows], c_mate))
        feed(1, lo, n)
    hid_copy = send(hid.at[1], hidr, c_mate)
    target_load.wait()
    xf[1, 0:WIN_TOK, :] = window_of(tt, t)
    point()
    xf[1, WIN_TOK:, :] = jnp.zeros((ROWS - WIN_TOK, D), F32)
    need(("near", 2))
    for copy in cnt_z:
        copy.wait_recv()
    count = (cnt[1] + cntr[1]) + (cntr[2] + cntr[3])
    count = count[0:1, 0:1]
    scaled_live = live * (token_total / count)
    e3 = []
    for i in range(2):
        if i == 1:
            need(("all", 2))
        es3[i] = shrunk(1, i).astype(BF16)
        e3.append(send(es3.at[i], er3.at[i], y_mate))
        acc[:, halves[i]] = mid[:, halves[i]] + shrink_row[:, halves[i]] + shrunk(0, i)

    e4 = []
    gr_c = []
    for i in range(2):
        cols = halves[i]
        e3[i].wait_recv()
        result = acc[:, cols] + er3[i].astype(F32)
        gap = result - xf[1, :, cols]
        grad = gap * scaled_live
        acc[:, cols] = grad
        gr[0, 0, :, cols] = grad.astype(BF16)
        e4.append(send(gr.at[0, 0, :, cols], gr.at[0, 1, :, cols], y_mate))
        gr_c.append(send(gr.at[0, 0, :, cols], gr.at[1, 0, :, cols], c_mate))
        bo[t, :, cols] = result.astype(BF16)
        sums[6:7, cols] = column_sum(gap * gap * live)
        sums[0:1, cols] = column_sum(grad)
    sb[0] = jnp.zeros((16, D), F32)
    sb[0, 6:7, :] = sums[6:7, :]
    sb[0, 0:1, :] = sums[0:1, :]

    def feed_back(w, lo, n):
        def body(j, carry):
            grad = dot_nn(gr[0, w, lo : lo + n, :], ws[j].reshape(D, D))
            grad = grad * slope[j, w, lo : lo + n, :]
            gb[j, w, lo : lo + n, :] = grad.astype(BF16)
            return carry

        lax.fori_loop(0, 2, body, 0)

    def expanded_back(w, lo, n):
        return dot_nt(gb[0, w, lo : lo + n, :], we[0].reshape(D, D)) + dot_nt(
            gb[1, w, lo : lo + n, :], we[1].reshape(D, D)
        )

    def rows_of(ref, width):
        return ref[...].reshape(2 * ROWS, width)

    def weight_grad(g, left, mine, theirs, width, at):
        def body(m, carry):
            cols = pl.ds(pl.multiple_of(m * 384, 128), 384)
            rows = pl.ds(m * 4, 4)
            value = dot_tn(left[0, :, :, cols].reshape(2 * ROWS, 384), mine.reshape(2 * ROWS, width))
            value = value + dot_tn(
                left[1, :, :, cols].reshape(2 * ROWS, 384), theirs.reshape(2 * ROWS, width)
            )
            gw[g, rows, :, at : at + width] = value.reshape(4, 96, width)
            return carry

        lax.fori_loop(0, 2, body, 0)

    to_x = {}
    to_z = {}

    pair_of = {}

    def pair_rows(k):
        return pl.ds(2 * z_mate(z, k), 2)

    def scatter_pairs(g):
        for i, k in enumerate((2, 1)):
            ps2[g, i] = gw[g, pair_rows(k), :, 640:768].astype(BF16)
            pair_of[g, i] = send(ps2.at[g, i], pr2.at[g, i], z_mates[0])

    parts = {0: ((0, 384), (384, 256)), 1: ((0, 640),), 2: ((0, 640),)}

    def scatter_blocks(g, i, blocks):
        lo, n = parts[g][i]
        for k in blocks:
            xs[g, k, :, lo : lo + n] = gw[g, row_of(k, 1 - x), :, lo : lo + n].astype(BF16)
            at = (g, k, slice(None), pl.ds(lo, n))
            to_x[g, k, i] = send(xs.at[at], xr.at[at], x_mate)

    def scatter_pair(g):
        pair_of[g, 0].wait_recv()
        total = gw[g, pair_rows(3), :, 640:768] + pr2[g, 0].astype(F32)
        ps2[g, 2] = total.astype(BF16)
        pair_of[g, 2] = send(ps2.at[g, 2], pr2.at[g, 2], z_mates[2])

    def scatter_turn(g):
        pair_of[g, 1].wait_recv()
        pair_of[g, 2].wait_recv()
        total = gw[g, pair_rows(0), :, 640:768] + pr2[g, 1].astype(F32)
        ptotal[g] = total + pr2[g, 2].astype(F32)
        pxs[g] = ptotal[g, 1 - x].astype(BF16)
        pair_of[g, 3] = send(pxs.at[g], pxr.at[g], x_mate)

    def scatter_z(g, k, i):
        lo, n = parts[g][i]
        cols = slice(lo, lo + n)
        to_x[g, k, i].wait_recv()
        total = gw[g, row_of(k, x), :, cols] + xr[g, k, :, cols].astype(F32)
        if k == 3:
            to_z[g, 2, i].wait_recv()
            total = total + zr[g, 1, :, cols].astype(F32)
        zs[g, k - 1, :, cols] = total.astype(BF16)
        at = (g, k - 1, slice(None), pl.ds(lo, n))
        to_z[g, k, i] = send(zs.at[at], zr.at[at], z_mates[2 if k == 3 else 0])

    def scatter_end(g, i, out):
        lo, n = parts[g][i]
        cols = slice(lo, lo + n)
        to_x[g, 0, i].wait_recv()
        to_z[g, 1, i].wait_recv()
        to_z[g, 3, i].wait_recv()
        total = gw[g, dp, :, cols] + xr[g, 0, :, cols].astype(F32)
        out[:, cols] = total + zr[g, 0, :, cols].astype(F32) + zr[g, 2, :, cols].astype(F32)

    def scatter_last(g, out):
        pair_of[g, 3].wait_recv()
        out[:, 640:768] = ptotal[g, x] + pxr[g].astype(F32)

    def scatter_add(g, *keys):
        steps = {"pair": scatter_pair, "turn": scatter_turn}
        for key in keys:
            if key in steps:
                add((key + "s", g), steps[key], g)
            else:
                add(("zs", g, *key), scatter_z, g, *key)

    for lo, n in CHUNKS:
        feed_back(0, lo, n)
    for i in range(2):
        e4[i].wait_recv()
        gr_c.append(send(gr.at[0, 1, :, halves[i]], gr.at[1, 1, :, halves[i]], c_mate))
    e5 = []
    for lo, n in CHUNKS:
        rows = pl.ds(lo, n)
        feed_back(1, lo, n)
        es[1, lo : lo + n, :] = expanded_back(1, lo, n).astype(BF16)
        e5.append(send(es.at[1, rows], er.at[1, rows], y_mate))
    gb_copy = send(gb.at[1], gbr, c_mate)
    mid[...] = expanded_back(0, 0, ROWS)
    for copy in gr_c:
        copy.wait_recv()
    hid_copy.wait_recv()
    weight_grad(2, gr, hid[0], hidr[...], D, 0)
    scatter_pairs(2)
    scatter_blocks(2, 0, (2, 3, 1, 0))
    scatter_add(2, "pair", (2, 0), "turn", (3, 0), (1, 0))
    point()

    e6 = []
    gm_c = []
    gain_part = jnp.zeros((1, D), F32)
    shift_part = jnp.zeros((1, D), F32)
    bias_part = jnp.zeros((1, D), F32)
    for i, (lo, n) in enumerate(CHUNKS):
        rows = pl.ds(lo, n)
        point()
        e5[i].wait_recv()
        grad = mid[lo : lo + n, :] + er[1, lo : lo + n, :].astype(F32)
        unit = unit2[lo : lo + n, :]
        gain_part = gain_part + column_sum(grad * unit)
        shift_part = shift_part + column_sum(grad)
        grad = acc[lo : lo + n, :] + normalize_back(grad, unit, inv2[lo : lo + n, :], gain2)
        acc[lo : lo + n, :] = grad
        gm[0, 0, lo : lo + n, :] = grad.astype(BF16)
        e6.append(send(gm.at[0, 0, rows], gm.at[0, 1, rows], y_mate))
        gm_c.append(send(gm.at[0, 0, rows], gm.at[1, 0, rows], c_mate))
        bias_part = bias_part + column_sum(grad)
    sb[0, 1:2, :] = gain_part
    sb[0, 2:3, :] = shift_part
    sb[0, 3:4, :] = bias_part

    bo_y = send(bo.at[t], bo.at[t], y_mate)
    bo_c = [send(bo.at[t], bo.at[t], c_mate)]

    def block_pass():
        bo_y.wait_recv()
        bo_c.append(send(bo.at[peer_window], bo.at[peer_window], c_mate))

    def block_mix():
        for copy in bo_c:
            copy.wait_recv()
        for w in range(4):
            mix[:, w, :] = bo[w, 0:WIN_TOK, :].astype(F32)
        xt[...] = mix[...].astype(BF16)
        stores.append(load(xt, block_out))

    stores = []
    gb_copy.wait_recv()
    for copy in n2_c:
        copy.wait_recv()
    weight_grad(1, n2, gb[0], gbr[...], D, 0)
    ones = jnp.ones((8, 2 * ROWS), BF16)
    sb[0, 8:9, :] = (dot_nn(ones, rows_of(gb.at[0], D)) + dot_nn(ones, rows_of(gbr, D)))[0:1]
    scatter_pairs(1)
    scatter_blocks(1, 0, (2, 3, 1, 0))
    scatter_add(1, "pair", (2, 0), "turn", (3, 0), (1, 0))
    point()

    def mixed_back(w, lo, n):
        for j in range(2):
            grad = dot_nn(gm[0, w, lo : lo + n, :], wa[j, :, :, 512:768].reshape(D, 256))
            gmx[j, w, lo : lo + n, :] = grad.astype(BF16)

    def unit_back(w, j, h):
        query, key, value = unit_of(w, j, h)
        p, pv = UNITS[h][3:]
        grad = gmx[j, w, :, 0:128] if h == 2 else gmx[j, w, :, 128:256]
        soft = ps[w, j, h]
        grad_soft = dot_nt(grad, value)
        delta = jnp.sum(soft * grad_soft, axis=-1, keepdims=True)
        grad_scores = (soft * (grad_soft - delta)).astype(BF16)
        grad_v = dot_tn(soft.astype(BF16), grad * half[pv])[0:ROWS]
        grad_k = dot_tn(grad_scores, query * key_mask[p])[0:ROWS]
        part = (dot_nt(grad_scores, pick[...]) * place[...]).astype(BF16)
        grad_q = dot_nn(grad_scores, key) + dot_nn(part, t2[p])
        tg[...] += dot_tn(query * half[p], part)
        return grad_q, grad_k, grad_v

    def attend_back_pair(w, j):
        one, two = unit_back(w, j, 0), unit_back(w, j, 1)
        for i in range(3):
            gp[j, w, :, 128 * i : 128 * i + 128] = (one[i] + two[i]).astype(BF16)

    def attend_back_last(w, j):
        grad_q, grad_k, grad_v = unit_back(w, j, 2)
        gp[j, w, :, 384:512] = (grad_q + pltpu.roll(grad_k, 64, 1)).astype(BF16)
        gp[j, w, :, 512:640] = pltpu.roll(grad_v, 64, 1).astype(BF16)

    def projected_back(w, lo, n):
        return dot_nt(gp[0, w, lo : lo + n, :], wa[0, :, :, 0:640].reshape(D, 640)) + dot_nt(
            gp[1, w, lo : lo + n, :], wa[1, :, :, 0:640].reshape(D, 640)
        )

    for i, (lo, n) in enumerate(CHUNKS):
        rows = pl.ds(lo, n)
        point()
        e6[i].wait_recv()
        gm_c.append(send(gm.at[0, 1, rows], gm.at[1, 1, rows], c_mate))
        mixed_back(1, lo, n)
    point()
    add(("block pass",), block_pass)
    add(("block mix",), block_mix)
    def both_back(j, carry):
        attend_back_pair(1, j)
        attend_back_last(1, j)
        return carry

    lax.fori_loop(0, 2, both_back, 0)
    point()
    gp_copies = [send(gp.at[1, 1], gpr.at[1], c_mate)]
    e7 = []
    for lo, n in CHUNKS:
        rows = pl.ds(lo, n)
        es[2, lo : lo + n, :] = projected_back(1, lo, n).astype(BF16)
        e7.append(send(es.at[2, rows], er.at[2, rows], y_mate))
    point()
    for copy in gm_c:
        copy.wait_recv()
    mx_copy.wait_recv()
    weight_grad(0, gm, mx[0], mxr[...], 256, 512)
    scatter_pairs(0)
    scatter_add(0, "pair", "turn")
    point()
    mixed_back(0, 0, ROWS)
    def pair_back(j, carry):
        attend_back_pair(0, j)
        return carry

    lax.fori_loop(0, 2, pair_back, 0)
    point()
    gp_copies.append(send(gp.at[1, 0, :, pl.ds(0, 384)], gpr.at[0, :, pl.ds(0, 384)], c_mate))
    attend_back_last(0, 0)
    point()
    n1_copy.wait_recv()
    for copy in gp_copies:
        copy.wait_recv()

    weight_grad(0, n1, gp[0, :, :, 0:384], gpr[:, :, 0:384], 384, 0)
    scatter_blocks(0, 0, (2, 3, 1, 0))
    scatter_add(0, (2, 0))
    attend_back_last(0, 1)
    last_copy = send(gp.at[1, 0, :, pl.ds(384, 256)], gpr.at[0, :, pl.ds(384, 256)], c_mate)
    mid[...] = projected_back(0, 0, ROWS)
    last_copy.wait_recv()
    held = gw[0, :, :, 512:640]
    weight_grad(0, n1, gp[0, :, :, 384:640], gpr[:, :, 384:640], 256, 384)
    gw[0, :, :, 512:640] += held
    need(("turns", 0))
    scatter_blocks(0, 1, (2, 3, 1, 0))

    small = {}

    def small_first():
        bias = dot_nn(ones, rows_of(gp.at[0], 640)) + dot_nn(ones, rows_of(gpr, 640))
        sb[0, 9:10, 0:640] = bias[0:1]
        spread = tg[...]
        spread_high = spread.astype(BF16)
        spread_low = (spread - spread_high.astype(F32)).astype(BF16)
        table = dot_nn(spread_high, onehot[...]) + dot_nn(spread_low, onehot[...])
        tb[0] = table[0:64] + table[64:128]

    top = pl.ds(0, 8)

    def small_send(stage, dst, mate, rows):
        return [
            send(sb.at[stage, rows], sbr.at[dst, rows], mate),
            send(tb.at[stage], tbr.at[dst], mate),
        ]

    def small_wait(stage):
        for copy in small[stage]:
            copy.wait_recv()

    def small_z():
        small[0] = sum((small_send(0, k - 1, z_mates[k - 1], pl.ds(0, 16)) for k in (1, 2, 3)), [])

    def small_c():
        small_wait(0)
        sb[1] = (sb[0] + sbr[0]) + (sbr[1] + sbr[2])
        tb[1] = (tb[0] + tbr[0]) + (tbr[1] + tbr[2])
        small[1] = small_send(1, 3, c_mate, top)

    def small_next(stage, mate, rows):
        small_wait(stage - 1)
        sb[stage] = sb[stage - 1]
        sb[stage, 0:8, :] = sb[stage - 1, 0:8, :] + sbr[stage + 1, 0:8, :]
        tb[stage] = tb[stage - 1] + tbr[stage + 1]
        small[stage] = small_send(stage, stage + 2, mate, rows)

    def small_end():
        small_wait(3)
        total = sb[3] + sbr[5]
        small_out[...] = total
        small_out[6:7, :] = jnp.broadcast_to(
            jnp.sum(total[6:7, :], axis=1, keepdims=True) / (count * float(D)), (1, D)
        )
        table_out[...] = (tb[3] + tbr[5]).T

    e8 = {}
    ig_c = {}

    def mix_in(window, i):
        lo, n = CHUNKS[i]
        top = min(lo + n, WIN_TOK)
        mix[lo:top, pl.ds(window, 1), :] = (
            ig[window, lo:top, :].astype(F32).reshape(top - lo, 1, D)
        )

    def own_grad(i):
        lo, n = CHUNKS[i]
        e7[i].wait_recv()
        grad = mid[lo : lo + n, :] + er[2, lo : lo + n, :].astype(F32)
        unit = unit1[lo : lo + n, :]
        gain_part = column_sum(grad * unit)
        shift_part = column_sum(grad)
        sb[0, 4:5, :] = gain_part if i == 0 else sb[0, 4:5, :] + gain_part
        sb[0, 5:6, :] = shift_part if i == 0 else sb[0, 5:6, :] + shift_part
        grad = acc[lo : lo + n, :] + normalize_back(grad, unit, inv1[lo : lo + n, :], gain1)
        ig[t, lo : lo + n, :] = grad.astype(BF16)
        rows = pl.ds(lo, n)
        ig_c[i, 0] = send(ig.at[t, rows], ig.at[t, rows], c_mate)
        e8[i] = send(ig.at[t, rows], ig.at[t, rows], y_mate)
        mix_in(t, i)

    def side_grad(i):
        ig_c[i, 0].wait_recv()
        mix_in(t + 1 - 2 * c, i)

    def peer_grad(i):
        lo, n = CHUNKS[i]
        rows = pl.ds(lo, n)
        e8[i].wait_recv()
        ig_c[i, 1] = send(ig.at[peer_window, rows], ig.at[peer_window, rows], c_mate)
        mix_in(peer_window, i)

    def last_grad(i):
        lo, n = CHUNKS[i]
        ig_c[i, 1].wait_recv()
        mix_in(peer_window + 1 - 2 * c, i)
        rows = pl.ds(lo, min(n, WIN_TOK - lo))
        stores.append(load(mix.at[rows], grad_out.at[rows]))

    def scatter_out(g, held, out):
        if g > 0:
            scatter_end(g, 0, held)
        else:
            scatter_end(0, 1, held)
        scatter_last(g, held)
        stores.append(load(held, out))

    need(("block mix",))
    add(("own", 0), own_grad, 0)
    add(("small first",), small_first)
    add(("own", 1), own_grad, 1)
    add(("small z",), small_z)
    scatter_add(0, (3, 0), (2, 1), (1, 0))
    add(("side", 0), side_grad, 0)
    add(("side", 1), side_grad, 1)
    add(("small c",), small_c)
    add(("out", 2), scatter_out, 2, gs, gs_out)
    add(("out", 1), scatter_out, 1, ge, ge_out)
    add(("small y",), small_next, 2, y_mate, top)
    add(("peer", 0), peer_grad, 0)
    scatter_add(0, (3, 1), (1, 1))
    add(("last", 0), last_grad, 0)
    add(("small x",), small_next, 3, x_mate, pl.ds(0, 16))
    add(("peer", 1), peer_grad, 1)
    add(("last", 1), last_grad, 1)
    add(("end", 0), scatter_end, 0, 0, ga)
    add(("out", 0), scatter_out, 0, ga, ga_out)
    add(("small end",), small_end)
    need(("small end",))
    for copy in started:
        copy.wait_send()
    for copy in stores:
        copy.wait()


def finish_kernel(
    block_in,
    grad_in,
    ga,
    ge,
    gs,
    small,
    table,
    block_out,
    loss_out,
    grad_out,
    gain1_out,
    shift1_out,
    triple_out,
    qv_out,
    out_w_out,
    out_b_out,
    gain2_out,
    shift2_out,
    we_out,
    expand_bias_out,
    ws_out,
    bias_shrink_out,
    rows_out,
    columns_out,
    block_hold,
    grad_hold,
    ge_hold,
    gs_hold,
    sems,
):
    moves = []
    at = 0
    for src, hold, dst, step in (
        (block_in, block_hold, block_out, 49),
        (grad_in, grad_hold, grad_out, 49),
        (ge, ge_hold, we_out, 96),
        (gs, gs_hold, ws_out, 96),
    ):
        for lo in range(0, src.shape[0], step):
            rows = pl.ds(lo, step)
            copy = pltpu.make_async_copy(src.at[rows], hold.at[rows], sems.at[at])
            copy.start()
            moves.append(
                (copy, pltpu.make_async_copy(hold.at[rows], dst.at[rows], sems.at[at + 1]))
            )
            at += 2
    for i in range(3):
        triple_out[i, :, 0:128] = ga[:, 128 * i : 128 * i + 128]
    triple_out[0, :, 128:192] = ga[:, 384:448]
    triple_out[1, :, 128:192] = pltpu.roll(ga[:, 384:512], 64, 1)[:, 0:64]
    triple_out[2, :, 128:192] = ga[:, 512:576]
    out_w_out[0:128, :] = ga[:, 640:768].T
    out_w_out[128:192, :] = ga[:, 512:640].T[64:128]
    loss_out[...] = small[6:7, 0:1]
    for i, out in enumerate(
        (bias_shrink_out, gain2_out, shift2_out, out_b_out, gain1_out, shift1_out)
    ):
        out[...] = small[i]
    expand_bias_out[...] = small[8]
    for i in range(2):
        qv_out[i : i + 1, 0:128] = small[9:10, 256 * i : 256 * i + 128]
        qv_out[i : i + 1, 128:192] = small[9:10, 384 + 128 * i : 448 + 128 * i]
    rows_out[...] = table[0:27]
    columns_out[...] = table[32:59]
    for arrive, leave in moves:
        arrive.wait()
        leave.start()
    for arrive, leave in moves:
        leave.wait()


def fused(
    inputs,
    target,
    valid,
    first_gain,
    first_shift,
    triple_weight,
    query_value_bias,
    output_weight,
    output_bias,
    second_gain,
    second_shift,
    expand_weight,
    expand_bias,
    shrink_weight,
    shrink_bias,
    rows_table,
    columns_table,
):
    vmem = pl.BlockSpec(memory_space=pltpu.VMEM)
    anywhere = pl.BlockSpec(memory_space=pl.ANY)
    mixed_shape = (WIN_TOK, 4, D)
    part = jax.ShapeDtypeStruct((96, D), F32)
    copies = 224
    parts = pl.pallas_call(
        block_kernel,
        out_shape=[
            jax.ShapeDtypeStruct(mixed_shape, BF16),
            jax.ShapeDtypeStruct(mixed_shape, F32),
            part,
            part,
            part,
            jax.ShapeDtypeStruct((16, D), F32),
            jax.ShapeDtypeStruct((64, 64), F32),
        ],
        in_specs=[anywhere] * 17,
        out_specs=[anywhere] * 5 + [vmem] * 2,
        scratch_shapes=[
            pltpu.VMEM(valid.shape, jnp.int32),
            pltpu.VMEM((D,), F32),
            pltpu.VMEM((D,), F32),
            pltpu.VMEM(triple_weight.shape, BF16),
            pltpu.VMEM(query_value_bias.shape, F32),
            pltpu.VMEM(output_weight.shape, BF16),
            pltpu.VMEM((D,), F32),
            pltpu.VMEM((D,), F32),
            pltpu.VMEM((D,), F32),
            pltpu.VMEM(expand_weight.shape, BF16),
            pltpu.VMEM(expand_bias.shape, F32),
            pltpu.VMEM(expand_weight.shape, BF16),
            pltpu.VMEM((D,), F32),
            pltpu.VMEM(rows_table.shape, F32),
            pltpu.VMEM(columns_table.shape, F32),
            pltpu.VMEM((96, D), BF16),
            pltpu.VMEM((2, 8, 96, D), BF16),
            pltpu.VMEM((2, 8, 96, D), BF16),
            pltpu.VMEM((2, 8, 96, D), BF16),
            pltpu.VMEM(mixed_shape, BF16),
            pltpu.VMEM(mixed_shape, BF16),
            pltpu.VMEM((512, 64), BF16),
            pltpu.VMEM((ROWS, 512), F32),
            pltpu.VMEM((512, KEYS), BF16),
            pltpu.VMEM((64, 128), F32),
            pltpu.VMEM((4, ROWS, D), BF16),
            pltpu.VMEM((4, ROWS, D), BF16),
            pltpu.VMEM(mixed_shape, F32),
            pltpu.VMEM((96, D), F32),
            pltpu.VMEM((96, D), F32),
            pltpu.VMEM((96, D), F32),
            pltpu.VMEM((2, 8, D), F32),
            pltpu.VMEM((2, ROWS, D), F32),
            pltpu.VMEM((ROWS, D), F32),
            pltpu.VMEM((ROWS, D), F32),
            pltpu.VMEM((ROWS, 1), F32),
            pltpu.VMEM((ROWS, 1), F32),
            pltpu.VMEM((ROWS, D), F32),
            pltpu.VMEM((ROWS, D), F32),
            pltpu.VMEM((2, 2, ROWS, D), BF16),
            pltpu.VMEM((2, 2, ROWS, D), BF16),
            pltpu.VMEM((2, 2, ROWS, D), BF16),
            pltpu.VMEM((2, 2, ROWS, D), BF16),
            pltpu.VMEM((2, 2, KEYS, 896), BF16),
            pltpu.VMEM((2, 2, 3, ROWS, KEYS), F32),
            pltpu.VMEM((2, 2, ROWS, 256), BF16),
            pltpu.VMEM((2, ROWS, 256), BF16),
            pltpu.VMEM((2, 2, ROWS, D), BF16),
            pltpu.VMEM((2, ROWS, D), BF16),
            pltpu.VMEM((2, 2, ROWS, D), F32),
            pltpu.VMEM((2, 2, ROWS, D), BF16),
            pltpu.VMEM((2, ROWS, D), BF16),
            pltpu.VMEM((2, 2, ROWS, 256), BF16),
            pltpu.VMEM((2, 2, ROWS, 640), BF16),
            pltpu.VMEM((2, ROWS, 640), BF16),
            pltpu.VMEM((2, 512, 128), BF16),
            pltpu.VMEM((128, 512), F32),
            pltpu.VMEM((3, ROWS, D), BF16),
            pltpu.VMEM((3, ROWS, D), BF16),
            pltpu.VMEM((2, ROWS, 384), BF16),
            pltpu.VMEM((2, ROWS, 384), BF16),
            pltpu.VMEM((8, D), F32),
            pltpu.VMEM((1, D), F32),
            pltpu.VMEM((3, 8, 96, D), F32),
            pltpu.VMEM((3, 4, 96, 640), BF16),
            pltpu.VMEM((3, 4, 96, 640), BF16),
            pltpu.VMEM((3, 3, 96, 640), BF16),
            pltpu.VMEM((3, 3, 96, 640), BF16),
            pltpu.VMEM((3, 3, 2, 96, 128), BF16),
            pltpu.VMEM((3, 3, 2, 96, 128), BF16),
            pltpu.VMEM((3, 2, 96, 128), F32),
            pltpu.VMEM((3, 96, 128), BF16),
            pltpu.VMEM((3, 96, 128), BF16),
            pltpu.VMEM((2, 8, 128), F32),
            pltpu.VMEM((4, 8, 128), F32),
            pltpu.VMEM((4, 16, D), F32),
            pltpu.VMEM((6, 16, D), F32),
            pltpu.VMEM((4, 64, 64), F32),
            pltpu.VMEM((6, 64, 64), F32),
            pltpu.SemaphoreType.DMA((32,)),
            pltpu.SemaphoreType.DMA((copies,)),
            pltpu.SemaphoreType.DMA((copies,)),
        ],
        compiler_params=pltpu.CompilerParams(
            collective_id=0, has_side_effects=True, vmem_limit_bytes=60 << 20
        ),
    )(
        inputs.transpose(1, 0, 2),
        target.transpose(1, 0, 2),
        valid,
        first_gain,
        first_shift,
        triple_weight,
        query_value_bias,
        output_weight,
        output_bias,
        second_gain,
        second_shift,
        expand_weight,
        expand_bias,
        shrink_weight.T,
        shrink_bias,
        rows_table,
        columns_table,
    )
    vector = jax.ShapeDtypeStruct((D,), F32)
    relative = jax.ShapeDtypeStruct(rows_table.shape, F32)
    outs = pl.pallas_call(
        finish_kernel,
        out_shape=[
            jax.ShapeDtypeStruct(mixed_shape, BF16),
            jax.ShapeDtypeStruct((1, 1), F32),
            jax.ShapeDtypeStruct(mixed_shape, F32),
            vector,
            vector,
            jax.ShapeDtypeStruct(triple_weight.shape, F32),
            jax.ShapeDtypeStruct(query_value_bias.shape, F32),
            jax.ShapeDtypeStruct(output_weight.shape, F32),
            vector,
            vector,
            vector,
            part,
            jax.ShapeDtypeStruct(expand_bias.shape, F32),
            part,
            vector,
            relative,
            relative,
        ],
        in_specs=[anywhere] * 2 + [vmem, anywhere, anywhere] + [vmem] * 2,
        out_specs=[
            anywhere if i in (0, 2, 11, 13) else vmem for i in range(17)
        ],
        scratch_shapes=[
            pltpu.VMEM(mixed_shape, BF16),
            pltpu.VMEM(mixed_shape, F32),
            pltpu.VMEM((96, D), F32),
            pltpu.VMEM((96, D), F32),
            pltpu.SemaphoreType.DMA((20,)),
        ],
    )(*parts)
    outs = list(outs)
    outs[0] = outs[0].transpose(1, 0, 2)
    outs[1] = outs[1].reshape(())
    outs[2] = outs[2].transpose(1, 0, 2)
    outs[13] = outs[13].T
    return tuple(outs)


def solution(mesh):
    placed = (
        P("dp", None, None),
        P("dp", None, None),
        P("dp", None),
        P(),
        P(),
        P(None, "dp", "tensor"),
        P(None, "tensor"),
        P("tensor", "dp"),
        P(),
        P(),
        P(),
        P("dp", "tensor"),
        P("tensor"),
        P("tensor", "dp"),
        P(),
        P(),
        P(),
    )
    on_slice = mesh.shape["dp"] == 8 and mesh.shape["tensor"] == 4
    return jax.shard_map(
        fused if on_slice else shards,
        mesh=mesh,
        in_specs=placed,
        out_specs=(
            P("dp", None, None),
            P(),
            P("dp", None, None),
            P(),
            P(),
            P(None, "dp", "tensor"),
            P(None, "tensor"),
            P("tensor", "dp"),
            P(),
            P(),
            P(),
            P("dp", "tensor"),
            P("tensor"),
            P("tensor", "dp"),
            P(),
            P(),
            P(),
        ),
        check_vma=False,
    )
```

profile of v0, /device:TPU:0, one launch (start us, length us, event | category | flops | bytes accessed | tf_op | source)
XLA Modules:
  0.0 132.6 jit_solution(9160154447467026803)
XLA Ops:
  0.7 126.2 %shard_map.296 = (bf16[196,4,768]{2,1,0:T(4,128)(2,1)}, f32[196,4,768]{2,1,0:T(4,128)}, f32[96,768]{1,0:T(8,128)}, f32[96,768]{1,0:T(8,128)}, f32[96,768]{1,0:T(...) custom-call(bf16[196,4,768]{2,1,0:T(4,128)(2,1)} %bitcast.7, bf16[196,4,768]{2,1,0:T(4,128)(2,1)} %bitcast.8, ...), custom_call_target="tpu_custom_call" | custom-call | tf_op jit(solution)/shard_map/pallas_call | solution.py:1440
  126.8 5.5 %shard_map.297 = (bf16[196,4,768]{2,1,0:T(4,128)(2,1)}, f32[1,1]{1,0:T(1,128)}, f32[196,4,768]{2,1,0:T(4,128)}, f32[768]{0:T(1024)}, f32[768]{0:T(1024)}, /*inde...) custom-call(bf16[196,4,768]{2,1,0:T(4,128)(2,1)} %get-tuple-element., ...), custom_call_target="tpu_custom_call" | custom-call | tf_op jit(solution)/shard_map/pallas_call | solution.py:1561
where the time goes:
time: 133 us
  Pallas kernels  132 us (99%)
    pallas_call x1, Pallas kernels, fused(): pl.pallas_call(block_kernel, out_shape=[jax.ShapeDtypeStruct(mixed_shape,...  126 us
    pallas_call x1, Pallas kernels, fused(): pl.pallas_call(finish_kernel, out_shape=[jax.ShapeDtypeStruct(mixed_shape...  5.53 us

commit v1 on v0

--- a/solution.py
+++ b/solution.py
@@ -413,7 +413,8 @@
 UNITS = ((0, 1, 2, 0, 0), (0, 1, 2, 1, 1), (3, 5, 6, 0, 1))
 
 
-PLAN = (2, 1, 3, 0, 1, 4, 1, 1, 1, 6, 1, 2, 0, 1, 2, 0, 0, 0, 0, 2, 1, 1, 2, 0, 1, 0, 0, 4, 2)
+ORDER = (('pair', 0, 0), ('x', 0, 0), ('z', 0, 3), ('far', 0), ('z', 0, 1), ('pair', 0, 3), ('count',), ('x', 0, 3), ('z', 0, 2), ('start', 1), ('pair', 0, 1), ('x', 0, 1), ('near', 0), ('pair', 0, 2), ('x', 0, 2), ('pair', 1, 0), ('all', 0), ('start', 2), ('z', 1, 3), ('pair', 1, 3), ('z', 1, 1), ('far', 1), ('x', 1, 0), ('z', 2, 3), ('pair', 1, 1), ('z', 1, 2), ('x', 1, 1), ('x', 1, 3), ('pair', 1, 2), ('pair', 2, 0), ('near', 1), ('x', 1, 2), ('z', 2, 1), ('all', 1), ('far', 2), ('pair', 2, 3), ('z', 2, 2), ('pair', 2, 1), ('x', 2, 0), ('x', 2, 1), ('near', 2), ('x', 2, 3), ('pair', 2, 2), ('x', 2, 2), ('all', 2), ('pairs', 2), ('zs', 2, 2, 0), ('turns', 2), ('zs', 2, 3, 0), ('zs', 2, 1, 0), ('pairs', 1), ('zs', 1, 2, 0), ('block pass',), ('zs', 1, 1, 0), ('pairs', 0), ('zs', 1, 3, 0), ('block mix',), ('zs', 0, 2, 0), ('own', 0), ('small first',), ('own', 1), ('small z',), ('side', 0), ('turns', 0), ('turns', 1), ('zs', 0, 2, 1), ('zs', 0, 1, 0), ('small c',), ('zs', 0, 3, 0), ('out', 1), ('out', 2), ('small y',), ('side', 1), ('peer', 0), ('zs', 0, 1, 1), ('zs', 0, 3, 1), ('small x',), ('end', 0), ('last', 0), ('peer', 1), ('last', 1), ('out', 0), ('small end',))
+PLAN = (0, 1, 1, 1, 2, 2, 3, 0, 0, 0, 1, 2, 1, 1, 1, 0, 0, 0, 0, 2, 0, 1, 3, 0, 1, 0, 1, 0, 3)
 
 
 def block_kernel(
@@ -651,6 +652,7 @@
 
     def add(key, step, *args):
         tasks.append((key, step, args))
+        tasks.sort(key=lambda task: ORDER.index(task[0]))
 
     def serve():
         key, step, args = tasks.pop(0)
@@ -736,7 +738,7 @@
     token = grid((ROWS, 512), 0)
     down, across = fourteens(token)
     hit = valid & (main == jnp.where(side_of > 0.5, across, down)) & (token < float(WIN_TOK))
-    place[...] = jnp.where(hit, 1.0, 0.0)
+    place[...] = jnp.where(hit, 1.0, 0.0).astype(BF16)
     side_of, main, other, valid = entries((512, KEYS), 0)
     token = grid((512, KEYS), 1)
     down, across = fourteens(token)
@@ -828,9 +830,10 @@
             mixes = []
             for h in range(3):
                 query, key, value = unit_of(w, j, h)
-                along = dot_nt(query, t2[UNITS[h][3]]) * place[...]
+                along = dot_nt(query, t2[UNITS[h][3]])
                 high = along.astype(BF16)
-                low = (along - high.astype(F32)).astype(BF16)
+                low = (along - high.astype(F32)).astype(BF16) * place[...]
+                high = high * place[...]
                 scores = dot_nt(query, key) + dot_nn(high, pick[...]) + dot_nn(low, pick[...])
                 scores = scores + key_bias
                 raised = jnp.exp(scores - jnp.max(scores, axis=-1, keepdims=True))
@@ -1136,7 +1139,7 @@
         grad_scores = (soft * (grad_soft - delta)).astype(BF16)
         grad_v = dot_tn(soft.astype(BF16), grad * half[pv])[0:ROWS]
         grad_k = dot_tn(grad_scores, query * key_mask[p])[0:ROWS]
-        part = (dot_nt(grad_scores, pick[...]) * place[...]).astype(BF16)
+        part = dot_nt(grad_scores, pick[...]).astype(BF16) * place[...]
         grad_q = dot_nn(grad_scores, key) + dot_nn(part, t2[p])
         tg[...] += dot_tn(query * half[p], part)
         return grad_q, grad_k, grad_v
@@ -1473,7 +1476,7 @@
             pltpu.VMEM(mixed_shape, BF16),
             pltpu.VMEM(mixed_shape, BF16),
             pltpu.VMEM((512, 64), BF16),
-            pltpu.VMEM((ROWS, 512), F32),
+            pltpu.VMEM((ROWS, 512), BF16),
             pltpu.VMEM((512, KEYS), BF16),
             pltpu.VMEM((64, 128), F32),
             pltpu.VMEM((4, ROWS, D), BF16),

time: 133 us -> 127 us (0.955)
  Pallas kernels: 132 us -> 126 us
    pallas_call x1, Pallas kernels: 126 us -> 120 us  [fused(): pl.pallas_call(block_kernel, out_shape=[jax.ShapeDtypeStruct(mixed_shape,...]
where the time goes in v1:
time: 127 us
  Pallas kernels  126 us (99%)
    pallas_call x1, Pallas kernels, fused(): pl.pallas_call(block_kernel, out_shape=[jax.ShapeDtypeStruct(mixed_shape,...  120 us
    pallas_call x1, Pallas kernels, fused(): pl.pallas_call(finish_kernel, out_shape=[jax.ShapeDtypeStruct(mixed_shape...  5.53 us

profile of v1, /device:TPU:0, one launch (start us, length us, event | category | flops | bytes accessed | tf_op | source)
XLA Modules:
  0.0 126.6 jit_solution(18046561990973617754)
XLA Ops:
  0.7 120.2 %shard_map.296 = (bf16[196,4,768]{2,1,0:T(4,128)(2,1)}, f32[196,4,768]{2,1,0:T(4,128)}, f32[96,768]{1,0:T(8,128)}, f32[96,768]{1,0:T(8,128)}, f32[96,768]{1,0:T(...) custom-call(bf16[196,4,768]{2,1,0:T(4,128)(2,1)} %bitcast.7, bf16[196,4,768]{2,1,0:T(4,128)(2,1)} %bitcast.8, ...), custom_call_target="tpu_custom_call" | custom-call | tf_op jit(solution)/shard_map/pallas_call | solution.py:1443
  120.9 5.5 %shard_map.297 = (bf16[196,4,768]{2,1,0:T(4,128)(2,1)}, f32[1,1]{1,0:T(1,128)}, f32[196,4,768]{2,1,0:T(4,128)}, f32[768]{0:T(1024)}, f32[768]{0:T(1024)}, /*inde...) custom-call(bf16[196,4,768]{2,1,0:T(4,128)(2,1)} %get-tuple-element., ...), custom_call_target="tpu_custom_call" | custom-call | tf_op jit(solution)/shard_map/pallas_call | solution.py:1564

commit v2 on v1

--- a/solution.py
+++ b/solution.py
@@ -926,29 +926,36 @@
     count = (cnt[1] + cntr[1]) + (cntr[2] + cntr[3])
     count = count[0:1, 0:1]
     scaled_live = live * (token_total / count)
+    pieces = [(0, 0, ROWS)] + [(1, lo, n) for lo, n in CHUNKS]
     e3 = []
     for i in range(2):
         if i == 1:
             need(("all", 2))
         es3[i] = shrunk(1, i).astype(BF16)
-        e3.append(send(es3.at[i], er3.at[i], y_mate))
+        for half_at, lo, n in pieces[:1] if i == 0 else pieces[1:]:
+            at = (i, pl.ds(lo, n))
+            e3.append(send(es3.at[at], er3.at[at], y_mate))
         acc[:, halves[i]] = mid[:, halves[i]] + shrink_row[:, halves[i]] + shrunk(0, i)
 
     e4 = []
     gr_c = []
-    for i in range(2):
-        cols = halves[i]
+    for i, (half_at, lo, n) in enumerate(pieces):
+        cols = halves[half_at]
+        part = slice(lo, lo + n)
+        rows = pl.ds(lo, n)
         e3[i].wait_recv()
-        result = acc[:, cols] + er3[i].astype(F32)
-        gap = result - xf[1, :, cols]
-        grad = gap * scaled_live
-        acc[:, cols] = grad
-        gr[0, 0, :, cols] = grad.astype(BF16)
-        e4.append(send(gr.at[0, 0, :, cols], gr.at[0, 1, :, cols], y_mate))
-        gr_c.append(send(gr.at[0, 0, :, cols], gr.at[1, 0, :, cols], c_mate))
-        bo[t, :, cols] = result.astype(BF16)
-        sums[6:7, cols] = column_sum(gap * gap * live)
-        sums[0:1, cols] = column_sum(grad)
+        result = acc[part, cols] + er3[half_at, part, :].astype(F32)
+        gap = result - xf[1, part, cols]
+        grad = gap * scaled_live[part, :]
+        acc[part, cols] = grad
+        gr[0, 0, part, cols] = grad.astype(BF16)
+        e4.append(send(gr.at[0, 0, rows, cols], gr.at[0, 1, rows, cols], y_mate))
+        gr_c.append(send(gr.at[0, 0, rows, cols], gr.at[1, 0, rows, cols], c_mate))
+        bo[t, part, cols] = result.astype(BF16)
+        lost = column_sum(gap * gap * live[part, :])
+        bias = column_sum(grad)
+        sums[6:7, cols] = lost if lo == 0 else sums[6:7, cols] + lost
+        sums[0:1, cols] = bias if lo == 0 else sums[0:1, cols] + bias
     sb[0] = jnp.zeros((16, D), F32)
     sb[0, 6:7, :] = sums[6:7, :]
     sb[0, 0:1, :] = sums[0:1, :]
@@ -1054,12 +1061,14 @@
 
     for lo, n in CHUNKS:
         feed_back(0, lo, n)
-    for i in range(2):
+    e5 = []
+    for i, (half_at, lo, n) in enumerate(pieces):
+        rows = pl.ds(lo, n)
+        cols = halves[half_at]
         e4[i].wait_recv()
-        gr_c.append(send(gr.at[0, 1, :, halves[i]], gr.at[1, 1, :, halves[i]], c_mate))
-    e5 = []
-    for lo, n in CHUNKS:
-        rows = pl.ds(lo, n)
+        gr_c.append(send(gr.at[0, 1, rows, cols], gr.at[1, 1, rows, cols], c_mate))
+        if i == 0:
+            continue
         feed_back(1, lo, n)
         es[1, lo : lo + n, :] = expanded_back(1, lo, n).astype(BF16)
         e5.append(send(es.at[1, rows], er.at[1, rows], y_mate))
@@ -1344,76 +1353,57 @@
         copy.wait()
 
 
-def finish_kernel(
-    block_in,
-    grad_in,
-    ga,
-    ge,
-    gs,
-    small,
-    table,
-    block_out,
-    loss_out,
-    grad_out,
-    gain1_out,
-    shift1_out,
-    triple_out,
-    qv_out,
-    out_w_out,
-    out_b_out,
-    gain2_out,
-    shift2_out,
-    we_out,
-    expand_bias_out,
-    ws_out,
-    bias_shrink_out,
-    rows_out,
-    columns_out,
-    block_hold,
-    grad_hold,
-    ge_hold,
-    gs_hold,
-    sems,
-):
-    moves = []
-    at = 0
+def finish_kernel(*refs):
+    block_in, grad_in, ga_in, ge, gs, small_in, table_in = refs[:7]
+    outs = refs[7:24]
+    block_hold, grad_hold, ge_hold, gs_hold, ga, small, table = refs[24:31]
+    held = refs[31:44]
+    sems = refs[44]
+    count = [0]
+
+    def move(src, dst):
+        copy = pltpu.make_async_copy(src, dst, sems.at[count[0]])
+        count[0] += 1
+        copy.start()
+        return copy
+
+    little = [move(src, dst) for src, dst in ((ga_in, ga), (small_in, small), (table_in, table))]
+    arrivals = []
     for src, hold, dst, step in (
-        (block_in, block_hold, block_out, 49),
-        (grad_in, grad_hold, grad_out, 49),
-        (ge, ge_hold, we_out, 96),
-        (gs, gs_hold, ws_out, 96),
+        (grad_in, grad_hold, outs[2], 49),
+        (block_in, block_hold, outs[0], 98),
+        (ge, ge_hold, outs[11], 96),
+        (gs, gs_hold, outs[13], 96),
     ):
         for lo in range(0, src.shape[0], step):
             rows = pl.ds(lo, step)
-            copy = pltpu.make_async_copy(src.at[rows], hold.at[rows], sems.at[at])
-            copy.start()
-            moves.append(
-                (copy, pltpu.make_async_copy(hold.at[rows], dst.at[rows], sems.at[at + 1]))
-            )
-            at += 2
+            arrivals.append((move(src.at[rows], hold.at[rows]), hold.at[rows], dst.at[rows]))
+    for copy in little:
+        copy.wait()
+    loss, gain1, shift1, triple, qv, out_w, out_b, gain2, shift2, expand_bias, shrink_bias, by_row, by_column = held
     for i in range(3):
-        triple_out[i, :, 0:128] = ga[:, 128 * i : 128 * i + 128]
-    triple_out[0, :, 128:192] = ga[:, 384:448]
-    triple_out[1, :, 128:192] = pltpu.roll(ga[:, 384:512], 64, 1)[:, 0:64]
-    triple_out[2, :, 128:192] = ga[:, 512:576]
-    out_w_out[0:128, :] = ga[:, 640:768].T
-    out_w_out[128:192, :] = ga[:, 512:640].T[64:128]
-    loss_out[...] = small[6:7, 0:1]
-    for i, out in enumerate(
-        (bias_shrink_out, gain2_out, shift2_out, out_b_out, gain1_out, shift1_out)
-    ):
+        triple[i, :, 0:128] = ga[:, 128 * i : 128 * i + 128]
+    triple[0, :, 128:192] = ga[:, 384:448]
+    triple[1, :, 128:192] = pltpu.roll(ga[:, 384:512], 64, 1)[:, 0:64]
+    triple[2, :, 128:192] = ga[:, 512:576]
+    out_w[0:128, :] = ga[:, 640:768].T
+    out_w[128:192, :] = ga[:, 512:640].T[64:128]
+    loss[...] = small[6:7, 0:1]
+    for i, out in enumerate((shrink_bias, gain2, shift2, out_b, gain1, shift1)):
         out[...] = small[i]
-    expand_bias_out[...] = small[8]
+    expand_bias[...] = small[8]
     for i in range(2):
-        qv_out[i : i + 1, 0:128] = small[9:10, 256 * i : 256 * i + 128]
-        qv_out[i : i + 1, 128:192] = small[9:10, 384 + 128 * i : 448 + 128 * i]
-    rows_out[...] = table[0:27]
-    columns_out[...] = table[32:59]
-    for arrive, leave in moves:
-        arrive.wait()
-        leave.start()
-    for arrive, leave in moves:
-        leave.wait()
+        qv[i : i + 1, 0:128] = small[9:10, 256 * i : 256 * i + 128]
+        qv[i : i + 1, 128:192] = small[9:10, 384 + 128 * i : 448 + 128 * i]
+    by_row[...] = table[0:27]
+    by_column[...] = table[32:59]
+    others = [out for i, out in enumerate(outs) if i not in (0, 2, 11, 13)]
+    leaving = [move(src, dst) for src, dst in zip(held, others, strict=True)]
+    for copy, hold, dst in arrivals:
+        copy.wait()
+        leaving.append(move(hold, dst))
+    for copy in leaving:
+        copy.wait()
 
 
 def fused(
@@ -1561,38 +1551,42 @@
     )
     vector = jax.ShapeDtypeStruct((D,), F32)
     relative = jax.ShapeDtypeStruct(rows_table.shape, F32)
+    shapes = [
+        jax.ShapeDtypeStruct(mixed_shape, BF16),
+        jax.ShapeDtypeStruct((1, 1), F32),
+        jax.ShapeDtypeStruct(mixed_shape, F32),
+        vector,
+        vector,
+        jax.ShapeDtypeStruct(triple_weight.shape, F32),
+        jax.ShapeDtypeStruct(query_value_bias.shape, F32),
+        jax.ShapeDtypeStruct(output_weight.shape, F32),
+        vector,
+        vector,
+        vector,
+        part,
+        jax.ShapeDtypeStruct(expand_bias.shape, F32),
+        part,
+        vector,
+        relative,
+        relative,
+    ]
+    small_shapes = [shape for i, shape in enumerate(shapes) if i not in (0, 2, 11, 13)]
     outs = pl.pallas_call(
         finish_kernel,
-        out_shape=[
-            jax.ShapeDtypeStruct(mixed_shape, BF16),
-            jax.ShapeDtypeStruct((1, 1), F32),
-            jax.ShapeDtypeStruct(mixed_shape, F32),
-            vector,
-            vector,
-            jax.ShapeDtypeStruct(triple_weight.shape, F32),
-            jax.ShapeDtypeStruct(query_value_bias.shape, F32),
-            jax.ShapeDtypeStruct(output_weight.shape, F32),
-            vector,
-            vector,
-            vector,
-            part,
-            jax.ShapeDtypeStruct(expand_bias.shape, F32),
-            part,
-            vector,
-            relative,
-            relative,
-        ],
-        in_specs=[anywhere] * 2 + [vmem, anywhere, anywhere] + [vmem] * 2,
-        out_specs=[
-            anywhere if i in (0, 2, 11, 13) else vmem for i in range(17)
-        ],
+        out_shape=shapes,
+        in_specs=[anywhere] * 7,
+        out_specs=[anywhere] * 17,
         scratch_shapes=[
             pltpu.VMEM(mixed_shape, BF16),
             pltpu.VMEM(mixed_shape, F32),
             pltpu.VMEM((96, D), F32),
             pltpu.VMEM((96, D), F32),
-            pltpu.SemaphoreType.DMA((20,)),
-        ],
+            pltpu.VMEM((96, D), F32),
+            pltpu.VMEM((16, D), F32),
+            pltpu.VMEM((64, 64), F32),
+        ]
+        + [pltpu.VMEM(shape.shape, shape.dtype) for shape in small_shapes]
+        + [pltpu.SemaphoreType.DMA((40,))],
     )(*parts)
     outs = list(outs)
     outs[0] = outs[0].transpose(1, 0, 2)

time: 127 us -> 124 us (0.976)
  Pallas kernels: 126 us -> 123 us
    pallas_call x1, Pallas kernels: 120 us -> 119 us  [fused(): pl.pallas_call(block_kernel, out_shape=[jax.ShapeDtypeStruct(mixed_shape,...]
    pallas_call x1, Pallas kernels: 5.53 us -> 4.19 us  [fused(): pl.pallas_call(finish_kernel, out_shape=shapes, in_specs=[anywhere] * 7,...]
where the time goes in v2:
time: 124 us
  Pallas kernels  123 us (99%)
    pallas_call x1, Pallas kernels, fused(): pl.pallas_call(block_kernel, out_shape=[jax.ShapeDtypeStruct(mixed_shape,...  119 us
    pallas_call x1, Pallas kernels, fused(): pl.pallas_call(finish_kernel, out_shape=shapes, in_specs=[anywhere] * 7,...  4.19 us

profile of v2, /device:TPU:0, one launch (start us, length us, event | category | flops | bytes accessed | tf_op | source)
XLA Modules:
  0.0 123.7 jit_solution(6718905303381672953)
XLA Ops:
  0.7 118.7 %shard_map.296 = (bf16[196,4,768]{2,1,0:T(4,128)(2,1)}, f32[196,4,768]{2,1,0:T(4,128)}, f32[96,768]{1,0:T(8,128)}, f32[96,768]{1,0:T(8,128)}, f32[96,768]{1,0:T(...) custom-call(bf16[196,4,768]{2,1,0:T(4,128)(2,1)} %bitcast.7, bf16[196,4,768]{2,1,0:T(4,128)(2,1)} %bitcast.8, ...), custom_call_target="tpu_custom_call" | custom-call | tf_op jit(solution)/shard_map/pallas_call | solution.py:1433
  119.3 4.2 %shard_map.297 = (bf16[196,4,768]{2,1,0:T(4,128)(2,1)}, f32[1,1]{1,0:T(1,128)}, f32[196,4,768]{2,1,0:T(4,128)}, f32[768]{0:T(1024)}, f32[768]{0:T(1024)}, /*inde...) custom-call(bf16[196,4,768]{2,1,0:T(4,128)(2,1)} %get-tuple-element., ...), custom_call_target="tpu_custom_call" | custom-call | tf_op jit(solution)/shard_map/pallas_call | solution.py:1574

commit v3 on v2

--- a/solution.py
+++ b/solution.py
@@ -1150,16 +1150,18 @@
         grad_k = dot_tn(grad_scores, query * key_mask[p])[0:ROWS]
         part = dot_nt(grad_scores, pick[...]).astype(BF16) * place[...]
         grad_q = dot_nn(grad_scores, key) + dot_nn(part, t2[p])
-        tg[...] += dot_tn(query * half[p], part)
-        return grad_q, grad_k, grad_v
+        spread = dot_tn(query * half[p], part)
+        return grad_q, grad_k, grad_v, spread
 
     def attend_back_pair(w, j):
         one, two = unit_back(w, j, 0), unit_back(w, j, 1)
         for i in range(3):
             gp[j, w, :, 128 * i : 128 * i + 128] = (one[i] + two[i]).astype(BF16)
+        tg[...] += one[3] + two[3]
 
     def attend_back_last(w, j):
-        grad_q, grad_k, grad_v = unit_back(w, j, 2)
+        grad_q, grad_k, grad_v, spread = unit_back(w, j, 2)
+        tg[...] += spread
         gp[j, w, :, 384:512] = (grad_q + pltpu.roll(grad_k, 64, 1)).astype(BF16)
         gp[j, w, :, 512:640] = pltpu.roll(grad_v, 64, 1).astype(BF16)
 

time: 124 us -> 124 us (level)
  no operation moved by 1% of the time
where the time goes in v3:
time: 124 us
  Pallas kernels  123 us (99%)
    pallas_call x1, Pallas kernels, fused(): pl.pallas_call(block_kernel, out_shape=[jax.ShapeDtypeStruct(mixed_shape,...  119 us
    pallas_call x1, Pallas kernels, fused(): pl.pallas_call(finish_kernel, out_shape=shapes, in_specs=[anywhere] * 7,...  4.19 us

profile of v3, /device:TPU:0, one launch (start us, length us, event | category | flops | bytes accessed | tf_op | source)
XLA Modules:
  0.0 123.7 jit_solution(683761398437407663)
XLA Ops:
  0.7 118.6 %shard_map.296 = (bf16[196,4,768]{2,1,0:T(4,128)(2,1)}, f32[196,4,768]{2,1,0:T(4,128)}, f32[96,768]{1,0:T(8,128)}, f32[96,768]{1,0:T(8,128)}, f32[96,768]{1,0:T(...) custom-call(bf16[196,4,768]{2,1,0:T(4,128)(2,1)} %bitcast.7, bf16[196,4,768]{2,1,0:T(4,128)(2,1)} %bitcast.8, ...), custom_call_target="tpu_custom_call" | custom-call | tf_op jit(solution)/shard_map/pallas_call | solution.py:1435
  119.3 4.2 %shard_map.297 = (bf16[196,4,768]{2,1,0:T(4,128)(2,1)}, f32[1,1]{1,0:T(1,128)}, f32[196,4,768]{2,1,0:T(4,128)}, f32[768]{0:T(1024)}, f32[768]{0:T(1024)}, /*inde...) custom-call(bf16[196,4,768]{2,1,0:T(4,128)(2,1)} %get-tuple-element., ...), custom_call_target="tpu_custom_call" | custom-call | tf_op jit(solution)/shard_map/pallas_call | solution.py:1576
